TPU v7x, 512 devices: a whole 4x4x16 slice. The times are simulated.
512 devices in a mesh: dp: 64 (over y, z), segment: 2 (over core), mp: 4 (over x).
Axes of the slice: x: 4, y: 4, z: 16, core: 2. Of those that a mesh axis runs over, the one named last changes fastest.
Arguments:
- hidden: bfloat16 [2, 512, 4096], P('segment', ('dp', 'mp')), may hold values from -6 to 6
- gain: float32 [4096], replicated, may hold values from 0.5 to 1.5
- head: bfloat16 [4096, 131072], P('segment', ('dp', 'mp')), may hold values from -0.09375 to 0.09375
- queries: bfloat16 [8, 131072], P(None, ('dp', 'mp')), may hold values from -48 to 48
- doc_spans: int32 [8], replicated, may hold values from 1 to 4, as said below
- labels: int32 [8], replicated, may hold values from 0 to 7
Outputs:
- grad_head: bfloat16 [4096, 131072], P('segment', ('dp', 'mp'))
- loss: float32 [], replicated
Inputs may be any that keep to these rules, and one draw needn't show every extreme that they name: `doc_spans`: the counts sum to 16; documents own consecutive spans in order; at least two documents have 4 spans.
All inputs are finite; a program needn't handle non-finite values.
Results may differ from a plain program's by a relative error of at most 0.008.
Values may be sent and summed in bfloat16 or wider, within the bound.
A program may use at most 64 MiB of HBM per device.

v0:
```python
import math
import jax
import jax.numpy as jnp
from jax import lax
from jax.sharding import PartitionSpec as P

V_DEV = 512
CH_MB = 8
NDOC = 8


def saturate(logits):
    return jnp.log1p(jax.nn.softplus(logits))


def slope(logits):
    return jax.nn.sigmoid(logits) / (1.0 + jax.nn.softplus(logits))


def row_norm(hidden, gain):
    values = hidden.astype(jnp.float32)
    mean_sq = jnp.mean(values * values, axis=-1, keepdims=True)
    return (values * lax.rsqrt(mean_sq + 1e-05) * gain).astype(jnp.bfloat16)


def owned_by(span_ids, bounds):
    inside = (span_ids[:, None] >= bounds[None, :-1]) & (span_ids[:, None] < bounds[None, 1:])
    return inside.astype(jnp.float32)


def shards(hidden, gain, head, queries, doc_spans, labels):
    width_dp = lax.axis_size("dp")
    width_mp = lax.axis_size("mp")
    segments = lax.axis_size("segment")
    vocab = V_DEV * width_dp * width_mp
    rows_here = hidden.shape[1]
    tok_mb = rows_here * width_dp * width_mp
    span = tok_mb // CH_MB
    micro_index = lax.axis_index("segment")
    normed = row_norm(hidden, gain)
    head_full = lax.all_gather(head, "segment", axis=0, tiled=True)
    bounds = jnp.concatenate([jnp.zeros((1,), jnp.int32), jnp.cumsum(doc_spans)])
    query_values = queries.astype(jnp.float32)
    scale = 1.0 / (math.sqrt(vocab) * span)

    def doc_table(count):
        span_ids = (micro_index * tok_mb + jnp.arange(count, dtype=jnp.int32)) // span
        return owned_by(span_ids, bounds)

    table = doc_table(tok_mb)
    rows = lax.all_gather(normed, ("dp", "mp"), axis=1, tiled=True)[0]
    block = jnp.dot(rows, head_full, preferred_element_type=jnp.float32)
    local_table = doc_table(rows.shape[0])
    pooled_now = jnp.dot(local_table.T, saturate(block), precision=lax.Precision.HIGHEST)
    pooled = pooled_now
    pooled = lax.psum(pooled, "segment")
    terms = jnp.dot(query_values, pooled.T, precision=lax.Precision.HIGHEST)
    scores = lax.psum(terms, ("dp", "mp")) * scale
    row_top = jnp.max(scores, axis=1, keepdims=True)
    log_total = row_top + jnp.log(jnp.sum(jnp.exp(scores - row_top), axis=1, keepdims=True))
    picks = (labels[:, None] == jnp.arange(NDOC, dtype=jnp.int32)[None, :]).astype(jnp.float32)
    loss = jnp.sum(log_total[:, 0] - jnp.sum(scores * picks, axis=1))
    score_grad = jnp.exp(scores - log_total) - picks
    pooled_grad = scale * jnp.dot(score_grad.T, query_values, precision=lax.Precision.HIGHEST)
    token_grad = jnp.dot(table, pooled_grad, precision=lax.Precision.HIGHEST)
    grad_scale = math.sqrt(vocab) * span / math.sqrt(segments * tok_mb)
    logit_grad = (token_grad * slope(block) * grad_scale).astype(jnp.bfloat16)
    rows = lax.all_gather(normed, ("dp", "mp"), axis=1, tiled=True)[0]
    summed = lax.dot_general(
        rows, logit_grad, (((0,), (0,)), ((), ())), preferred_element_type=jnp.float32
    )
    grad_head = lax.psum_scatter(
        summed.astype(jnp.bfloat16), "segment", scatter_dimension=0, tiled=True
    )
    return (grad_head, loss)


def solution(mesh):
    return jax.shard_map(
        shards,
        mesh=mesh,
        in_specs=(
            P("segment", ("dp", "mp"), None),
            P(),
            P("segment", ("dp", "mp")),
            P(None, ("dp", "mp")),
            P(),
            P(),
        ),
        out_specs=(P("segment", ("dp", "mp")), P()),
        check_vma=False,
    )
```

profile of v0, /device:TPU:1, one launch (start us, length us, event | category | flops | bytes accessed | tf_op | source)
XLA Modules:
  0.0 1000.5 jit_solution(7330918718881482748)
XLA Ops:
  7.2 0.0 copy-start
  7.2 0.0 all-gather.5.cloned.1.call-start
  7.2 0.7 all-gather.5.cloned.1.call-update
  7.9 0.0 all-gather.3.cloned.1.call-start
  8.0 0.9 fusion.16
  8.8 0.8 fusion.18
  9.7 0.6 copy.10
  10.3 0.0 all-gather.3.cloned.1.call-update
  10.3 0.0 reduce-scatter.2.cloned.1.call-start
  10.4 0.8 reduce-window.8
  11.2 0.1 pad_add_fusion
  11.3 0.0 copy-start.1
  11.3 29.7 %all-gather.5.cloned.1.call-done = bf16[4096,512]{1,0:T(8,128)(2,1)} async-done(((bf16[2048,512]{1,0:T(8,128)(2,1)}), bf16[4096,512]{1,0:T(8,128)(2,1)}) %all-gather.5.cloned.1.call-update) | async-done | bytes 4194320 | tf_op jit(solution)/shard_map/all_gather | solution.py:41
  41.0 216.8 %all-gather.3.cloned.1.call-done = bf16[1,512,4096]{2,0,1:T(2,128)(2,1)} async-done(((bf16[1,2,4096]{2,0,1:T(2,128)(2,1)}), bf16[1,512,4096]{2,0,1:T(2,128)(2,1)}) %all-gather.3.cloned.1.call-update) | async-done | bytes 4194320 | tf_op jit(solution)/shard_map/all_gather | solution.py:68
  257.8 9.3 fusion.1
  267.1 1.4 fusion.7
  268.5 11.3 %psum.14 = f32[8,512]{1,0:T(8,128)S(1)} all-reduce(f32[8,512]{1,0:T(8,128)S(1)} %fusion.7), channel_id=1, replica_groups=mesh['dp'=64,'segment'=2,'mp'=4] {'segment'}, use_global_device_ids=true, to_apply=%region_2.3 | all-reduce | flops 4096 | bytes 32768 | tf_op jit(solution)/shard_map/psum | solution.py:56
  279.7 0.0 copy-done
  279.7 0.1 convolution_bitcast_fusion
  279.9 577.1 %psum.15 = f32[8,8]{0,1:T(8,128)S(1)} all-reduce(f32[8,8]{0,1:T(8,128)S(1)} %convolution_bitcast_fusion), channel_id=1, replica_groups=mesh['dp'=64,'segment'=2,'mp'=4] {'dp','mp'}, use_global_device_ids=true, to_apply=%region_3.4 | all-reduce | flops 64 | bytes 512 | tf_op jit(solution)/shard_map/psum | solution.py:58
  857.0 0.0 copy-done.1
  857.0 0.6 subtract_reduce_fusion
  857.6 0.1 convolution_multiply_fusion.1
  857.7 1.4 fusion.6
  859.1 14.9 %convolution_convert_fusion = bf16[4096,512]{1,0:T(8,128)(2,1)} fusion(bf16[512,512]{1,0:T(8,128)(2,1)S(1)} %fusion.6, bf16[1,512,4096]{2,0,1:T(2,128)(2,1)} %all-gather.3.cloned.1.call-done), kind=kOutput, calls=%fused_computation | convolution fusion | flops 2149580800 | bytes 8912896 | tf_op jit(solution)/shard_map/dot_general | solution.py:69
  874.0 0.0 reduce-scatter.2.cloned.1.call-update
  874.0 119.9 %reduce-scatter.2.cloned.1.call-done = bf16[2048,512]{1,0:T(8,128)(2,1)} async-done(((bf16[4096,512]{1,0:T(8,128)(2,1)}), bf16[2048,512]{1,0:T(8,128)(2,1)}) %reduce-scatter.2.cloned.1.call-update) | async-done | bytes 2097168 | tf_op jit(solution)/shard_map/reduce_scatter | solution.py:72
  (4 shorter events, 0.1 us)
Async XLA Ops:
  7.2 272.6 %copy-start = (bf16[8,512]{1,0:T(8,128)(2,1)S(1)}, bf16[8,512]{1,0:T(8,128)(2,1)}, u32[]{:S(2)}) copy-start(bf16[8,512]{1,0:T(8,128)(2,1)} %param.9) | copy-start | bytes 24580
  7.2 33.8 %all-gather.5.cloned.1.call-start = ((), (), s32[]{:S(2)}) async-start(), calls=%async_computation.2 | async-start | bytes 6291456 | tf_op jit(solution)/shard_map/all_gather | solution.py:41
  7.9 249.9 %all-gather.3.cloned.1.call-start = ((), (), s32[]{:S(2)}) async-start(), calls=%async_computation.1 | async-start | bytes 8421376 | tf_op jit(solution)/shard_map/all_gather | solution.py:68
  10.3 983.7 %reduce-scatter.2.cloned.1.call-start = ((), (), s32[]{:S(2)}) async-start(), calls=%async_computation.3 | async-start | bytes 6291456 | tf_op jit(solution)/shard_map/reduce_scatter | solution.py:72
  11.3 845.7 %copy-start.1 = (s32[8]{0:T(128)S(1)}, s32[8]{0:T(128)}, u32[]{:S(2)}) copy-start(s32[8]{0:T(128)} %param.11) | copy-start | bytes 100
Sparse Core Ops, SparseCore 0:
  10.1 30.8 all-gather.4
  46.2 211.6 all-gather.2
  874.2 119.7 reduce-scatter.1
where the time goes:
time: 1000 us
  blocking collectives  588 us (59%)
  waiting for transfers between devices  367 us (37%)
  matrix products  27.1 us (3%)
  between operations  13.8 us (1%)
    psum x1, blocking collectives, shards(): scores = lax.psum(terms, ('dp', 'mp')) * scale  577 us
    all_gather x1, waiting for transfers between devices, shards(): rows = lax.all_gather(normed, ('dp', 'mp'), axis=1, tiled=True)[0]  217 us
    reduce_scatter x1, waiting for transfers between devices, shards(): lax.psum_scatter(summed.astype(jnp.bfloat16), 'segment', scatter_dimensio...  120 us
    all_gather x1, waiting for transfers between devices, shards(): head_full = lax.all_gather(head, 'segment', axis=0, tiled=True)  29.7 us
  transfers between devices with their start and end apart: 3, of which 3 were waited for; matrix products, arithmetic and copies ran while one was open for 0% of the time, Pallas kernels for 0%

commit v1 on v0

--- a/solution.py
+++ b/solution.py
@@ -55,7 +55,7 @@
     pooled = pooled_now
     pooled = lax.psum(pooled, "segment")
     terms = jnp.dot(query_values, pooled.T, precision=lax.Precision.HIGHEST)
-    scores = lax.psum(terms, ("dp", "mp")) * scale
+    scores = lax.psum(lax.psum(terms, "mp"), "dp") * scale
     row_top = jnp.max(scores, axis=1, keepdims=True)
     log_total = row_top + jnp.log(jnp.sum(jnp.exp(scores - row_top), axis=1, keepdims=True))
     picks = (labels[:, None] == jnp.arange(NDOC, dtype=jnp.int32)[None, :]).astype(jnp.float32)

time: 1000 us -> 466 us (0.47)
  blocking collectives: 588 us -> 133 us
  waiting for transfers between devices: 367 us -> 288 us
    psum x1 -> x2, blocking collectives: 577 us -> 121 us  [shards(): scores = lax.psum(lax.psum(terms, 'mp'), 'dp') * scale]
    reduce_scatter x1, waiting for transfers between devices: 120 us -> 40.3 us  [shards(): lax.psum_scatter(summed.astype(jnp.bfloat16), 'segment', scatter_dimensio...]
  transfers between devices with their start and end apart: 3 -> 3, of which waited for: 3 -> 3; matrix products, arithmetic and copies ran while one was open for 0% -> 1% of each run, Pallas kernels for 0% -> 0%
where the time goes in v1:
time: 466 us; the launch traced here: 465 us
  waiting for transfers between devices  288 us (62%)
  blocking collectives  133 us (29%)
  matrix products  27.1 us (6%)
  between operations  13.8 us (3%)
    all_gather x1, waiting for transfers between devices, shards(): rows = lax.all_gather(normed, ('dp', 'mp'), axis=1, tiled=True)[0]  217 us
    psum x2, blocking collectives, shards(): scores = lax.psum(lax.psum(terms, 'mp'), 'dp') * scale  121 us
    reduce_scatter x1, waiting for transfers between devices, shards(): lax.psum_scatter(summed.astype(jnp.bfloat16), 'segment', scatter_dimensio...  40.3 us
    all_gather x1, waiting for transfers between devices, shards(): head_full = lax.all_gather(head, 'segment', axis=0, tiled=True)  29.7 us
    dot_general x1, matrix products, shards(): lax.dot_general(rows, logit_grad, (((0,), (0,)), ((), ())), preferred_ele...  14.9 us
    psum x1, blocking collectives, shards(): pooled = lax.psum(pooled, 'segment')  11.3 us
  transfers between devices with their start and end apart: 3, of which 3 were waited for; matrix products, arithmetic and copies ran while one was open for 1% of the time, Pallas kernels for 0%

profile of v1, /device:TPU:1, one launch (start us, length us, event | category | flops | bytes accessed | tf_op | source)
XLA Modules:
  0.0 465.1 jit_solution(4058266175011190773)
XLA Ops:
  7.2 0.0 copy-start
  7.2 0.0 all-gather.5.cloned.1.call-start
  7.2 0.7 all-gather.5.cloned.1.call-update
  7.9 0.0 all-gather.3.cloned.1.call-start
  8.0 0.9 fusion.16
  8.8 0.8 fusion.18
  9.7 0.6 copy.10
  10.3 0.0 all-gather.3.cloned.1.call-update
  10.3 0.0 reduce-scatter.2.cloned.1.call-start
  10.4 0.8 reduce-window.8
  11.2 0.1 pad_add_fusion
  11.3 0.0 copy-start.1
  11.3 29.7 %all-gather.5.cloned.1.call-done = bf16[4096,512]{1,0:T(8,128)(2,1)} async-done(((bf16[2048,512]{1,0:T(8,128)(2,1)}), bf16[4096,512]{1,0:T(8,128)(2,1)}) %all-gather.5.cloned.1.call-update) | async-done | bytes 4194320 | tf_op jit(solution)/shard_map/all_gather | solution.py:41
  41.0 216.8 %all-gather.3.cloned.1.call-done = bf16[1,512,4096]{2,0,1:T(2,128)(2,1)} async-done(((bf16[1,2,4096]{2,0,1:T(2,128)(2,1)}), bf16[1,512,4096]{2,0,1:T(2,128)(2,1)}) %all-gather.3.cloned.1.call-update) | async-done | bytes 4194320 | tf_op jit(solution)/shard_map/all_gather | solution.py:68
  257.8 9.3 %fusion.1 = f32[512,512]{1,0:T(8,128)S(1)} fusion(bf16[4096,512]{1,0:T(8,128)(2,1)} %all-gather.5.cloned.1.call-done, bf16[1,512,4096]{2,0,1:T(2,128)(2,1)} %all-gather.3.cloned.1.call-done), kind=kOutput, calls=%fused_computation.2 | convolution fusion | flops 2147483648 | bytes 9437184 | tf_op jit(solution)/shard_map/dot_general | solution.py:52
  267.1 1.4 fusion.7
  268.5 11.3 %psum.21 = f32[8,512]{1,0:T(8,128)S(1)} all-reduce(f32[8,512]{1,0:T(8,128)S(1)} %fusion.7), channel_id=1, replica_groups=mesh['dp'=64,'segment'=2,'mp'=4] {'segment'}, use_global_device_ids=true, to_apply=%region_2.3 | all-reduce | flops 4096 | bytes 32768 | tf_op jit(solution)/shard_map/psum | solution.py:56
  279.7 0.0 copy-done
  279.7 0.1 convolution_bitcast_fusion
  279.9 7.8 %psum.22 = f32[8,8]{0,1:T(8,128)S(1)} all-reduce(f32[8,8]{0,1:T(8,128)S(1)} %convolution_bitcast_fusion), channel_id=1, replica_groups=mesh['dp'=64,'segment'=2,'mp'=4] {'mp'}, use_global_device_ids=true, to_apply=%region_3.4 | all-reduce | flops 64 | bytes 512 | tf_op jit(solution)/shard_map/psum | solution.py:58
  287.6 113.5 %psum.23 = f32[8,8]{0,1:T(8,128)S(1)} all-reduce(f32[8,8]{0,1:T(8,128)S(1)} %psum.22), channel_id=1, replica_groups=mesh['dp'=64,'segment'=2,'mp'=4] {'dp'}, use_global_device_ids=true, to_apply=%region_4.5 | all-reduce | flops 64 | bytes 512 | tf_op jit(solution)/shard_map/psum | solution.py:58
  401.1 0.0 copy-done.1
  401.2 0.6 subtract_reduce_fusion
  401.8 0.1 convolution_multiply_fusion.1
  401.9 1.4 fusion.6
  403.3 14.9 %convolution_convert_fusion = bf16[4096,512]{1,0:T(8,128)(2,1)} fusion(bf16[512,512]{1,0:T(8,128)(2,1)S(1)} %fusion.6, bf16[1,512,4096]{2,0,1:T(2,128)(2,1)} %all-gather.3.cloned.1.call-done), kind=kOutput, calls=%fused_computation | convolution fusion | flops 2149580800 | bytes 8912896 | tf_op jit(solution)/shard_map/dot_general | solution.py:69
  418.2 0.0 reduce-scatter.2.cloned.1.call-update
  418.2 40.3 %reduce-scatter.2.cloned.1.call-done = bf16[2048,512]{1,0:T(8,128)(2,1)} async-done(((bf16[4096,512]{1,0:T(8,128)(2,1)}), bf16[2048,512]{1,0:T(8,128)(2,1)}) %reduce-scatter.2.cloned.1.call-update) | async-done | bytes 2097168 | tf_op jit(solution)/shard_map/reduce_scatter | solution.py:72
  (4 shorter events, 0.1 us)
Async XLA Ops:
  7.2 272.6 %copy-start = (bf16[8,512]{1,0:T(8,128)(2,1)S(1)}, bf16[8,512]{1,0:T(8,128)(2,1)}, u32[]{:S(2)}) copy-start(bf16[8,512]{1,0:T(8,128)(2,1)} %param.9) | copy-start | bytes 24580
  7.2 33.8 %all-gather.5.cloned.1.call-start = ((), (), s32[]{:S(2)}) async-start(), calls=%async_computation.2 | async-start | bytes 6291456 | tf_op jit(solution)/shard_map/all_gather | solution.py:41
  7.9 249.9 %all-gather.3.cloned.1.call-start = ((), (), s32[]{:S(2)}) async-start(), calls=%async_computation.1 | async-start | bytes 8421376 | tf_op jit(solution)/shard_map/all_gather | solution.py:68
  10.3 448.2 %reduce-scatter.2.cloned.1.call-start = ((), (), s32[]{:S(2)}) async-start(), calls=%async_computation.3 | async-start | bytes 6291456 | tf_op jit(solution)/shard_map/reduce_scatter | solution.py:72
  11.3 389.8 %copy-start.1 = (s32[8]{0:T(128)S(1)}, s32[8]{0:T(128)}, u32[]{:S(2)}) copy-start(s32[8]{0:T(128)} %param.11) | copy-start | bytes 100
Sparse Core Ops, SparseCore 0:
  10.1 30.8 all-gather.4
  46.2 211.6 all-gather.2
  418.3 40.1 reduce-scatter.1

commit v2 on v0

--- a/solution.py
+++ b/solution.py
@@ -65,7 +65,10 @@
     token_grad = jnp.dot(table, pooled_grad, precision=lax.Precision.HIGHEST)
     grad_scale = math.sqrt(vocab) * span / math.sqrt(segments * tok_mb)
     logit_grad = (token_grad * slope(block) * grad_scale).astype(jnp.bfloat16)
-    rows = lax.all_gather(normed, ("dp", "mp"), axis=1, tiled=True)[0]
+    rows = jnp.concatenate(
+        lax.all_to_all(jnp.stack([normed] * lax.axis_size(("dp", "mp"))), ("dp", "mp"), 0, 0),
+        axis=1,
+    )[0]
     summed = lax.dot_general(
         rows, logit_grad, (((0,), (0,)), ((), ())), preferred_element_type=jnp.float32
     )

time: 1000 us -> 1060 us (1.060)
  starting transfers between devices: 0.12 us -> 26.8 us
  waiting for transfers between devices: 367 us -> 392 us
  local copies, waits for them, and re-layouts: 0.66 us -> 13.5 us
    all_to_all x0 -> x1, starting transfers between devices: none -> 26.5 us  [shards(): lax.all_to_all(jnp.stack([normed] * lax.axis_size(('dp', 'mp'))), ('dp',...]
    all_gather x1, waiting for transfers between devices: 217 us -> 243 us  [shards(): rows = lax.all_gather(normed, ('dp', 'mp'), axis=1, tiled=True)[0]]
    another operation x0 -> x2, local copies, waits for them, and re-layouts: none -> 13.4 us  [the longest x1 7.21 us: shards(): jnp.concatenate(lax.all_to_all(jnp.stack([normed] * lax.axis_size(('dp',...]
  transfers between devices with their start and end apart: 3 -> 4, of which waited for: 3 -> 3; matrix products, arithmetic and copies ran while one was open for 0% -> 1% of each run, Pallas kernels for 0% -> 0%
where the time goes in v2:
time: 1060 us
  blocking collectives  588 us (55%)
  waiting for transfers between devices  392 us (37%)
  starting transfers between devices  26.8 us (3%)
  matrix products  18.8 us (2%)
  between operations  13.8 us (1%)
  local copies, waits for them, and re-layouts  13.5 us (1%)
    psum x1, blocking collectives, shards(): scores = lax.psum(terms, ('dp', 'mp')) * scale  577 us
    all_gather x1, waiting for transfers between devices, shards(): rows = lax.all_gather(normed, ('dp', 'mp'), axis=1, tiled=True)[0]  243 us
    reduce_scatter x1, waiting for transfers between devices, shards(): lax.psum_scatter(summed.astype(jnp.bfloat16), 'segment', scatter_dimensio...  120 us
    all_gather x1, waiting for transfers between devices, shards(): head_full = lax.all_gather(head, 'segment', axis=0, tiled=True)  27.2 us
    all_to_all x1, starting transfers between devices, shards(): lax.all_to_all(jnp.stack([normed] * lax.axis_size(('dp', 'mp'))), ('dp',...  26.5 us
  transfers between devices with their start and end apart: 4, of which 3 were waited for; matrix products, arithmetic and copies ran while one was open for 1% of the time, Pallas kernels for 0%

profile of v2, /device:TPU:1, one launch (start us, length us, event | category | flops | bytes accessed | tf_op | source)
XLA Modules:
  0.0 1055.4 jit_solution(17185608308409426427)
XLA Ops:
  7.2 0.0 copy-start
  7.2 0.9 multiply_reduce_fusion
  8.0 0.8 multiply_convert_fusion
  8.9 0.0 copy-start.1
  8.9 6.2 stack.2
  15.1 0.0 copy-start.3
  15.1 0.0 copy-done.1
  15.1 26.5 %all-to-all-start = ((bf16[256,1,2,4096]{3,2,1,0:T(2,128)(2,1)}), bf16[256,1,2,4096]{3,2,1,0:T(2,128)(2,1)}, u32[]{:S(2)}, u32[]{:S(2)}) async-start(bf16[256,1,2,4096]{3,2,1,0:T(2,128)(2,1)} %stack.2), calls=%async_computation | async-start | bytes 8388608 | tf_op jit(solution)/shard_map/all_to_all | solution.py:69
  41.7 0.0 all-gather.5.cloned.1.call-start
  41.8 0.7 all-gather.5.cloned.1.call-update
  42.4 0.0 all-gather.3.cloned.1.call-start
  42.5 0.7 all-gather.3.cloned.1.call-update
  43.2 0.2 reduce-scatter.2.cloned.1.call-start
  43.4 0.0 copy-done.3
  43.4 0.2 reduce-window.8
  43.6 0.1 pad_add_fusion
  43.7 0.0 copy-start.2
  43.7 27.2 %all-gather.5.cloned.1.call-done = bf16[4096,512]{1,0:T(8,128)(2,1)} async-done(((bf16[2048,512]{1,0:T(8,128)(2,1)}), bf16[4096,512]{1,0:T(8,128)(2,1)}) %all-gather.5.cloned.1.call-update) | async-done | bytes 4194320 | tf_op jit(solution)/shard_map/all_gather | solution.py:41
  70.9 243.1 %all-gather.3.cloned.1.call-done = bf16[1,512,4096]{2,0,1:T(2,128)(2,1)} async-done(((bf16[1,2,4096]{2,0,1:T(2,128)(2,1)}), bf16[1,512,4096]{2,0,1:T(2,128)(2,1)}) %all-gather.3.cloned.1.call-update) | async-done | bytes 4194320 | tf_op jit(solution)/shard_map/all_gather | solution.py:51
  314.0 9.3 fusion
  323.3 1.4 fusion.5
  324.7 11.3 %psum.14 = f32[8,512]{1,0:T(8,128)S(1)} all-reduce(f32[8,512]{1,0:T(8,128)S(1)} %fusion.5), channel_id=1, replica_groups=mesh['dp'=64,'segment'=2,'mp'=4] {'segment'}, use_global_device_ids=true, to_apply=%region_2.3 | all-reduce | flops 4096 | bytes 32768 | tf_op jit(solution)/shard_map/psum | solution.py:56
  335.9 0.0 copy-done
  335.9 0.1 convolution_bitcast_fusion
  336.1 576.9 %psum.15 = f32[8,8]{0,1:T(8,128)S(1)} all-reduce(f32[8,8]{0,1:T(8,128)S(1)} %convolution_bitcast_fusion), channel_id=1, replica_groups=mesh['dp'=64,'segment'=2,'mp'=4] {'dp','mp'}, use_global_device_ids=true, to_apply=%region_3.4 | all-reduce | flops 64 | bytes 512 | tf_op jit(solution)/shard_map/psum | solution.py:58
  913.0 0.0 copy-done.2
  913.0 0.6 subtract_reduce_fusion
  913.6 0.1 convolution_multiply_fusion.1
  913.8 1.4 fusion.4
  915.1 0.0 all-to-all-done
  915.1 7.2 squeeze_reshape.3
  922.4 6.5 convolution_convert_fusion
  928.9 0.0 reduce-scatter.2.cloned.1.call-update
  928.9 119.9 %reduce-scatter.2.cloned.1.call-done = bf16[2048,512]{1,0:T(8,128)(2,1)} async-done(((bf16[4096,512]{1,0:T(8,128)(2,1)}), bf16[2048,512]{1,0:T(8,128)(2,1)}) %reduce-scatter.2.cloned.1.call-update) | async-done | bytes 2097168 | tf_op jit(solution)/shard_map/reduce_scatter | solution.py:75
  (5 shorter events, 0.1 us)
Async XLA Ops:
  7.2 328.8 %copy-start = (bf16[8,512]{1,0:T(8,128)(2,1)S(1)}, bf16[8,512]{1,0:T(8,128)(2,1)}, u32[]{:S(2)}) copy-start(bf16[8,512]{1,0:T(8,128)(2,1)} %param.9) | copy-start | bytes 24580
  8.9 6.3 copy-start.1
  15.1 28.3 %copy-start.3 = (s32[8]{0:T(128)S(1)}, s32[8]{0:T(128)}, u32[]{:S(2)}) copy-start(s32[8]{0:T(128)} %param.10) | copy-start | bytes 100
  15.1 900.0 %all-to-all-start = ((bf16[256,1,2,4096]{3,2,1,0:T(2,128)(2,1)}), bf16[256,1,2,4096]{3,2,1,0:T(2,128)(2,1)}, u32[]{:S(2)}, u32[]{:S(2)}) async-start(bf16[256,1,2,4096]{3,2,1,0:T(2,128)(2,1)} %stack.2), calls=%async_computation | async-start | bytes 8388608 | tf_op jit(solution)/shard_map/all_to_all | solution.py:69
  41.7 29.2 %all-gather.5.cloned.1.call-start = ((), (), s32[]{:S(2)}) async-start(), calls=%async_computation.3 | async-start | bytes 6291456 | tf_op jit(solution)/shard_map/all_gather | solution.py:41
  42.4 271.6 %all-gather.3.cloned.1.call-start = ((), (), s32[]{:S(2)}) async-start(), calls=%async_computation.2 | async-start | bytes 8421376 | tf_op jit(solution)/shard_map/all_gather | solution.py:51
  43.2 1005.7 %reduce-scatter.2.cloned.1.call-start = ((), (), s32[]{:S(2)}) async-start(), calls=%async_computation.4 | async-start | bytes 6291456 | tf_op jit(solution)/shard_map/reduce_scatter | solution.py:75
  43.7 869.3 %copy-start.2 = (s32[8]{0:T(128)S(1)}, s32[8]{0:T(128)}, u32[]{:S(2)}) copy-start(s32[8]{0:T(128)} %param.11) | copy-start | bytes 100
Sparse Core Ops, SparseCore 0:
  44.6 26.2 all-gather.4
  76.1 237.9 all-gather.2
  929.1 119.7 reduce-scatter.1
